TPU v7x, 32 devices: a whole 2x2x4 slice. The times are simulated.
32 devices in a mesh: grp: 2 (over x), blk: 16 (over z, y, core).
Axes of the slice: x: 2, y: 2, z: 4, core: 2. Of those that a mesh axis runs over, the one named last changes fastest.
Arguments:
- observed: bfloat16 [512, 16384], P(('grp', 'blk')), parts along dimension 0, may hold values from 0.03 to 2.1, as said below
- good_pixel_mask: int32 [512, 16384], P(('grp', 'blk')), parts along dimension 0, may hold values from 0 to 1, as said below
- templates: bfloat16 [512, 65632], P(('grp', 'blk')), parts along dimension 0, may hold values from -6 to 6
- template_kernel_index: int32 [512], P(('grp', 'blk')), parts along dimension 0, may hold values from 0 to 7
- line_spread_table: float32 [8, 97], replicated, may hold values from 0.05 to 1
- exposure_per_row: int32 [512], P('grp'), parts along dimension 0, may hold values from 0 to 255, each once
Outputs:
- ccf: float32 [512, 16384], P('grp', 'blk'), parts along dimension 0
There are 2 independent parts, one for each index of `grp`. A program takes and returns all parts, laid end to end along the dimension named above; an argument that names none is the same for every part. Nothing has to cross between parts.
Inputs may be any that keep to these rules, and one draw needn't show every extreme that they name: observed flux is positive, so masked is above zero exactly on good pixels. `good_pixel_mask`: some pixel columns are bad in every exposure.
All inputs are finite; a program needn't handle non-finite values.
Results may differ from a plain program's by a relative error of at most 0.0015.
Values may be sent and summed in bfloat16 or wider, within the bound.
A program may use at most 128 MiB of HBM per device.

v0:
```python
import functools
import math

import jax
import jax.numpy as jnp
from jax import lax
from jax.experimental import pallas as pl
from jax.experimental.pallas import tpu as pltpu
from jax.sharding import PartitionSpec as P

PIX = 16384
LAGS = 64
TAPS = 97
KERNELS = 8
Q = 128
R = PIX // Q
BAND = 640
CHUNKS = 8
AHEAD = 1
F32 = jnp.float32
BF16 = jnp.bfloat16
MESH = pl.DeviceIdType.MESH
NT_DIMS = (((1,), (1,)), ((), ()))


def template_kernel(index_ref, table_ref, templates_ref, x_ref, bands, chunks, smooth):
    count = templates_ref.shape[0]
    spread_templates(table_ref, templates_ref, bands, chunks)
    smooth_templates(index_ref, bands, chunks, smooth, 0, count, count)
    pack_templates(smooth, x_ref, count)


def spread_templates(table_ref, templates_ref, bands, chunks):
    count = templates_ref.shape[0]
    for k in range(KERNELS):
        row = jnp.concatenate(
            [table_ref[k : k + 1, :], jnp.zeros((1, BAND - TAPS), F32)], axis=1
        )
        row = jnp.broadcast_to(row, (Q, BAND))
        band = pltpu.roll(row, 0, 1, stride=4, stride_axis=0)
        high = band.astype(BF16)
        bands[k, :, :BAND] = high
        bands[k, :, BAND:] = (band - high.astype(F32)).astype(BF16)

    def spread(r, _):
        at = pl.multiple_of(r * (4 * Q), 128)
        piece = templates_ref[:, pl.ds(at, BAND)].astype(F32)
        for i in range(BAND // 128):
            chunks[i, pl.ds(pl.multiple_of(r * count, count), count), :] = piece[
                :, 128 * i : 128 * (i + 1)
            ]
        return 0

    lax.fori_loop(0, R - 1, spread, 0, unroll=8)
    last = (R - 1) * 4 * Q
    left = templates_ref.shape[1] - last
    tail = templates_ref[:, last:].astype(F32)
    tail = jnp.concatenate([tail, jnp.zeros((count, BAND - left), F32)], axis=1)
    for i in range(BAND // 128):
        chunks[i, (R - 1) * count :, :] = tail[:, 128 * i : 128 * (i + 1)]


def smooth_templates(index_ref, bands, chunks, smooth, first, last, count):
    for t in range(first, last):
        rows = [
            chunks[i, pl.ds(t, R, stride=count), :].astype(BF16) for i in range(BAND // 128)
        ]
        rows = jnp.concatenate(rows + rows, axis=1)
        flux = lax.dot_general(
            bands[index_ref[t]], rows, NT_DIMS, preferred_element_type=F32
        )
        total = jnp.sum(flux * flux)
        smooth[pl.ds(t, Q, stride=count), :] = flux * lax.rsqrt(
            jnp.full((1, 1), total) / PIX + 1e-06
        )


def pack_templates(smooth, x_ref, count):
    half = LAGS // 2
    body = smooth[...]
    lane = lax.broadcasted_iota(jnp.int32, (half * count, R), 1)
    x_ref[half * count : (half + Q) * count, :] = body.astype(BF16)
    before = pltpu.roll(body[(Q - half) * count :, :], 1, 1)
    x_ref[: half * count, :] = jnp.where(lane == 0, 0.0, before).astype(BF16)
    after = pltpu.roll(body[: half * count, :], R - 1, 1)
    x_ref[(half + Q) * count :, :] = jnp.where(lane == R - 1, 0.0, after).astype(BF16)


def shape_templates(templates, template_kernel_index, line_spread_table):
    count = templates.shape[0]
    return pl.pallas_call(
        template_kernel,
        out_shape=jax.ShapeDtypeStruct(((Q + LAGS) * count, R), BF16),
        in_specs=[
            pl.BlockSpec(memory_space=pltpu.SMEM),
            pl.BlockSpec(memory_space=pltpu.VMEM),
            pl.BlockSpec(memory_space=pltpu.VMEM),
        ],
        out_specs=pl.BlockSpec(memory_space=pltpu.VMEM),
        scratch_shapes=[
            pltpu.VMEM((KERNELS, Q, 2 * BAND), BF16),
            pltpu.VMEM((BAND // 128, R * count, 128), F32),
            pltpu.VMEM((Q * count, R), F32),
        ],
        compiler_params=pltpu.CompilerParams(vmem_limit_bytes=40 * 2**20),
        cost_estimate=pl.CostEstimate(
            flops=2 * count * Q * R * 2 * BAND, bytes_accessed=6 * 2**20, transcendentals=0
        ),
        name="shape_templates",
    )(template_kernel_index, line_spread_table, templates)


def place_rows(rows_ref, acc, out_ref, count):
    total_rows = rows_ref.shape[1]
    chosen = (
        lax.broadcasted_iota(jnp.int32, (total_rows, total_rows), 0) == rows_ref[...]
    ).astype(BF16)
    both = jnp.concatenate([chosen, chosen], axis=1)
    for t in range(0, count, 2):
        part = jnp.concatenate(
            [
                jnp.concatenate(
                    [
                        acc[h, pl.ds(t + i, LAGS, stride=count), :]
                        for h in range(total_rows // 128)
                    ],
                    axis=1,
                )
                for i in range(2)
            ],
            axis=0,
        ) * F32(1.0 / math.sqrt(PIX))
        high = part.astype(BF16)
        low = (part - high.astype(F32)).astype(BF16)
        out_ref[:, t * LAGS : (t + 2) * LAGS] = lax.dot_general(
            both,
            jnp.concatenate([high, low], axis=1),
            NT_DIMS,
            preferred_element_type=F32,
        )


def correlate_kernel(step_q, rows_ref, x_ref, g_ref, out_ref, acc):
    step = pl.program_id(0)
    total_rows = rows_ref.shape[1]
    count = x_ref.shape[0] // (Q + LAGS)
    tile = 256

    @pl.when(step == 0)
    def _():
        acc[...] = jnp.zeros_like(acc)

    right = jnp.concatenate([g_ref[i] for i in range(step_q)], axis=1)
    for m in range(LAGS * count // tile):
        left = jnp.concatenate(
            [
                x_ref[pl.ds(pl.multiple_of((step * step_q + i) * count + m * tile, 16), tile), :]
                for i in range(step_q)
            ],
            axis=1,
        )
        part = lax.dot_general(left, right, NT_DIMS, preferred_element_type=F32)
        for h in range(total_rows // 128):
            acc[h, m * tile : (m + 1) * tile, :] += part[:, 128 * h : 128 * (h + 1)]

    @pl.when(step == pl.num_programs(0) - 1)
    def _():
        place_rows(rows_ref, acc, out_ref, count)


def correlate(x, gathered, exposure_per_row):
    total_rows = gathered.shape[1]
    count = x.shape[0] // (Q + LAGS)
    step_q = 8
    return pl.pallas_call(
        functools.partial(correlate_kernel, step_q),
        grid=(Q // step_q,),
        out_shape=jax.ShapeDtypeStruct((total_rows, count * LAGS), F32),
        in_specs=[
            pl.BlockSpec((1, total_rows), lambda s: (0, 0)),
            pl.BlockSpec(x.shape, lambda s: (0, 0)),
            pl.BlockSpec((step_q, total_rows, R), lambda s: (s, 0, 0)),
        ],
        out_specs=pl.BlockSpec((total_rows, count * LAGS), lambda s: (0, 0)),
        scratch_shapes=[pltpu.VMEM((total_rows // 128, LAGS * count, 128), F32)],
        compiler_params=pltpu.CompilerParams(vmem_limit_bytes=40 * 2**20),
        name="correlate",
    )(exposure_per_row.reshape(1, total_rows), x, gathered)


def mean_kernel(
    n,
    part_ref,
    index_ref,
    table_ref,
    templates_ref,
    mean_ref,
    x_ref,
    slots,
    own_mean,
    send_sem,
    recv_sem,
    bands,
    chunks,
    smooth,
):
    count = templates_ref.shape[0]
    me = lax.axis_index("blk")
    barrier = pltpu.get_barrier_semaphore()

    def greet(o, _):
        pl.semaphore_signal(
            barrier, inc=1, device_id={"blk": lax.rem(me + o, n)}, device_id_type=MESH
        )
        return 0

    lax.fori_loop(1, n, greet, 0)
    pl.semaphore_wait(barrier, n - 1)

    def part_copy(o):
        to = lax.rem(me + o, n)
        return pltpu.make_async_remote_copy(
            src_ref=part_ref.at[to],
            dst_ref=slots.at[o],
            send_sem=send_sem.at[0, o],
            recv_sem=recv_sem.at[0, o],
            device_id={"blk": to},
            device_id_type=MESH,
        )

    def mean_copy(o):
        return pltpu.make_async_remote_copy(
            src_ref=own_mean,
            dst_ref=mean_ref.at[me],
            send_sem=send_sem.at[1, o],
            recv_sem=recv_sem.at[1, o],
            device_id={"blk": lax.rem(me + o, n)},
            device_id_type=MESH,
        )

    for o in range(1, n):
        part_copy(o).start()
    spread_templates(table_ref, templates_ref, bands, chunks)
    smooth_templates(index_ref, bands, chunks, smooth, 0, count // 2, count)
    total = part_ref[me]
    for o in range(1, n):
        part_copy(o).wait_recv()
        total = total + slots[o]
    own_mean[...] = total[0] / jnp.maximum(total[1], 1.0)
    for o in range(1, n):
        mean_copy(o).start()
    mean_ref[me] = own_mean[...]
    smooth_templates(index_ref, bands, chunks, smooth, count // 2, count, count)
    pack_templates(smooth, x_ref, count)
    for o in range(1, n):
        mean_copy(o).wait_recv()
    for o in range(1, n):
        part_copy(o).wait_send()
        mean_copy(o).wait_send()


def column_means(sums, counts, n, templates, template_kernel_index, line_spread_table):
    part = jnp.stack([sums.reshape(n, -1, 128), counts.reshape(n, -1, 128)], axis=1)
    share = part.shape[2]
    count = templates.shape[0]
    mean, x = pl.pallas_call(
        functools.partial(mean_kernel, n),
        out_shape=(
            jax.ShapeDtypeStruct((n, share, 128), F32),
            jax.ShapeDtypeStruct(((Q + LAGS) * count, R), BF16),
        ),
        in_specs=[
            pl.BlockSpec(memory_space=pltpu.VMEM),
            pl.BlockSpec(memory_space=pltpu.SMEM),
            pl.BlockSpec(memory_space=pltpu.VMEM),
            pl.BlockSpec(memory_space=pltpu.VMEM),
        ],
        out_specs=(pl.BlockSpec(memory_space=pltpu.VMEM), pl.BlockSpec(memory_space=pltpu.VMEM)),
        scratch_shapes=[
            pltpu.VMEM((n, 2, share, 128), F32),
            pltpu.VMEM((share, 128), F32),
            pltpu.SemaphoreType.DMA((2, n)),
            pltpu.SemaphoreType.DMA((2, n)),
            pltpu.VMEM((KERNELS, Q, 2 * BAND), BF16),
            pltpu.VMEM((BAND // 128, R * count, 128), F32),
            pltpu.VMEM((Q * count, R), F32),
        ],
        compiler_params=pltpu.CompilerParams(
            collective_id=0, has_side_effects=True, vmem_limit_bytes=40 * 2**20
        ),
        name="column_means",
    )(part, template_kernel_index, line_spread_table, templates)
    return mean.reshape(-1), x


def gather_kernel(chunks, ready_ref, x_ref, acc_ref, held, send_sem, recv_sem):
    me = lax.axis_index("blk")
    z, y, c = me // 4, (me // 2) % 2, me % 2
    span = Q // chunks
    count = x_ref.shape[0] // (Q + LAGS)
    rows = ready_ref.shape[1]
    planes, total_rows = 4, 16 * rows
    tile = 256

    def blk(zz, yy, cc):
        return (zz * 2 + yy) * 2 + cc

    up, down = blk(z + 1, y, c), blk(z - 1, y, c)
    beside, twin = blk(z, 1 - y, c), blk(z, y, 1 - c)

    middle = (z == 1) | (z == 2)
    barrier = pltpu.get_barrier_semaphore()

    def greet(to):
        pl.semaphore_signal(barrier, inc=1, device_id={"blk": to}, device_id_type=MESH)

    greet(beside)
    greet(twin)
    pl.when(z < planes - 1)(lambda: greet(up))
    pl.when(z > 0)(lambda: greet(down))
    held[me] = ready_ref[...]
    acc_ref[...] = jnp.zeros_like(acc_ref)
    inner = (z > 0).astype(jnp.int32) + (z < planes - 1).astype(jnp.int32)
    pl.semaphore_wait(barrier, 2 + inner)

    def copy(source, k, slot, to):
        part = held.at[source, pl.ds(k * span, span)]
        return pltpu.make_async_remote_copy(
            src_ref=part,
            dst_ref=part,
            send_sem=send_sem.at[slot, k],
            recv_sem=recv_sem.at[source, k],
            device_id={"blk": to},
            device_id_type=MESH,
        )

    def z_part(h, k, sign, finish):
        zs = z - sign * h
        source = blk(zs, y, c)

        def go():
            if h > 0 and not finish:
                copy(source, k, 0, twin).wait_recv()

            def act(slot, to):
                one = copy(source, k, slot, to)
                if finish:
                    one.wait_send()
                else:
                    one.start()

            if sign > 0 or h == 0:
                pl.when(z < planes - 1)(lambda: act(zs, up))
            if sign < 0 or h == 0:
                pl.when(z > 0)(lambda: act(4 + zs, down))
            skip = (zs == 3 * (1 - z % 2)) & (middle | (k % 2 == 1))
            pl.when(jnp.logical_not(skip))(lambda: act(8 + zs, beside))
            act(12 + zs, twin)

        if h == 0:
            go()
        else:
            pl.when((zs >= 0) & (zs < planes))(go)

    def y_part(h, k, sign, finish):
        zs = z - sign * h
        source = blk(zs, 1 - y, c)

        def go():
            one = copy(source, k, 16 + zs, twin)
            along = copy(source, k, 20, jnp.where(z % 2 == 0, up, down))
            passes = (zs == 3 * (z % 2)) & (jnp.logical_not(middle) | (k % 2 == 1))
            if finish:
                one.wait_send()
                pl.when(passes)(lambda: along.wait_send())
            else:
                one.wait_recv()
                pl.when(passes)(lambda: along.start())
                one.start()

        if h == 0:
            go()
        else:
            pl.when((zs >= 0) & (zs < planes))(go)

    def each_hop(part, k_of, finish):
        for h in range(planes):
            k = k_of(h)

            @pl.when((k >= 0) & (k < chunks))
            def _():
                part(h, k, 1, finish)
                if h > 0:
                    part(h, k, -1, finish)

    def product(k):
        for zy in range(2 * planes):
            copy(zy * 2 + 1 - c, k, 0, twin).wait_recv()
        right = jnp.concatenate(
            [held[:, k * span + i].reshape(total_rows, R) for i in range(span)], axis=1
        )

        def one_tile(m, _):
            left = jnp.concatenate(
                [
                    x_ref[pl.ds(pl.multiple_of((k * span + i) * count + m * tile, 16), tile), :]
                    for i in range(span)
                ],
                axis=1,
            )
            acc_ref[pl.ds(pl.multiple_of(m * tile, tile), tile), :] += lax.dot_general(
                left, right, NT_DIMS, preferred_element_type=F32
            )
            return 0

        for m in range(LAGS * count // tile):
            one_tile(m, 0)

    lag = planes + 1 + AHEAD

    def step(s, _):
        each_hop(z_part, lambda h: s - h - (AHEAD if h > 0 else 0), False)
        each_hop(y_part, lambda h: s - h - 1 - AHEAD, False)
        pl.when(s >= lag)(lambda: product(s - lag))
        return 0

    lax.fori_loop(0, chunks + lag, step, 0)

    def finish(k, _):
        each_hop(z_part, lambda h: k, True)
        each_hop(y_part, lambda h: k, True)
        return 0

    lax.fori_loop(0, chunks, finish, 0)


def gather_correlate(x, ready):
    rows = ready.shape[1]
    count = x.shape[0] // (Q + LAGS)
    chunks = CHUNKS
    return pl.pallas_call(
        functools.partial(gather_kernel, chunks),
        out_shape=jax.ShapeDtypeStruct((LAGS * count, 16 * rows), F32),
        in_specs=[pl.BlockSpec(memory_space=pltpu.VMEM)] * 2,
        out_specs=pl.BlockSpec(memory_space=pltpu.VMEM),
        scratch_shapes=[
            pltpu.VMEM((16, Q, rows, R), BF16),
            pltpu.SemaphoreType.DMA((21, chunks)),
            pltpu.SemaphoreType.DMA((16, chunks)),
        ],
        compiler_params=pltpu.CompilerParams(
            collective_id=1, has_side_effects=True, vmem_limit_bytes=40 * 2**20
        ),
        name="gather_correlate",
    )(ready, x)


def place_kernel(rows_ref, acc_ref, out_ref, split):
    total_rows = rows_ref.shape[1]
    count = acc_ref.shape[0] // LAGS
    for h in range(total_rows // 128):
        split[h] = acc_ref[:, 128 * h : 128 * (h + 1)]
    place_rows(rows_ref, split, out_ref, count)


def place(acc, exposure_per_row):
    total_rows = acc.shape[1]
    return pl.pallas_call(
        place_kernel,
        out_shape=jax.ShapeDtypeStruct((total_rows, acc.shape[0]), F32),
        in_specs=[pl.BlockSpec(memory_space=pltpu.VMEM)] * 2,
        out_specs=pl.BlockSpec(memory_space=pltpu.VMEM),
        scratch_shapes=[pltpu.VMEM((total_rows // 128, acc.shape[0], 128), F32)],
        compiler_params=pltpu.CompilerParams(vmem_limit_bytes=16 * 2**20),
        name="place",
    )(exposure_per_row.reshape(1, total_rows), acc)


def shards(
    devices,
    observed,
    good_pixel_mask,
    templates,
    template_kernel_index,
    line_spread_table,
    exposure_per_row,
):
    rows = observed.shape[0]
    ring = devices == 16 and rows % 16 == 0
    good = good_pixel_mask > 0
    flux = jnp.where(good, observed, 0).astype(F32)
    present = (flux > 0).astype(F32)
    sums, counts = jnp.sum(flux, axis=0), jnp.sum(present, axis=0)
    if ring:
        mean, x = column_means(
            sums, counts, devices, templates, template_kernel_index, line_spread_table
        )
    else:
        x = shape_templates(templates, template_kernel_index, line_spread_table)
        sums = lax.psum(jnp.stack([sums, counts]), "blk")
        mean = sums[0] / jnp.maximum(sums[1], 1.0)
    resid = present * (flux - mean[None, :])
    scale = lax.rsqrt(jnp.sum(resid * resid, axis=1) / PIX + 1e-06)
    ready = (resid * scale[:, None]).astype(BF16)
    ready = ready.reshape(rows, R, Q).transpose(2, 0, 1)
    if ring:
        return place(gather_correlate(x, ready), exposure_per_row)
    gathered = lax.all_gather(ready, "blk", axis=1, tiled=True)
    return correlate(x, gathered, exposure_per_row)


def solution(mesh):
    in_specs = (
        P(("grp", "blk"), None),
        P(("grp", "blk"), None),
        P(("grp", "blk"), None),
        P(("grp", "blk")),
        P(),
        P("grp"),
    )
    out_specs = P("grp", "blk")
    return jax.shard_map(
        functools.partial(shards, mesh.shape["blk"]),
        mesh=mesh,
        in_specs=in_specs,
        out_specs=out_specs,
        check_vma=False,
    )
```

profile of v0, /device:TPU:0, one launch (start us, length us, event | category | flops | bytes accessed | tf_op | source)
XLA Modules:
  0.0 71.7 jit_solution(1949928076680299085)
XLA Ops:
  0.0 0.0 copy-start.1
  0.0 0.0 copy-start.3
  0.0 0.0 copy-start
  0.0 2.0 %convert_reduce_fusion = (f32[16384]{0:T(1024)S(1)}, f32[16384]{0:T(1024)S(1)}, bf16[16,16384]{1,0:T(8,128)(2,1)S(1)}) fusion(bf16[16,16384]{1,0:T(8,128)(2,1)} %param.6, s32[16,16384]{1,0:T(8,128)} %param.7), kind=kLoop, calls=%fused_computation.1 | loop fusion | flops 1802240 | bytes 2228224 | tf_op jit(solution)/shard_map/reduce_sum | solution.py:493
  2.0 0.0 copy-done.1
  2.0 0.0 copy-done.3
  2.0 0.0 copy-done
  2.1 16.6 %column_means.1 = (f32[16,8,128]{2,1,0:T(8,128)S(1)}, bf16[3072,128]{1,0:T(8,128)(2,1)S(1)}) custom-call(f32[16,2,8,128]{3,2,1,0:T(8,128)S(1)} %pad_maximum_fusion.part_ref, s32[16]{0:T(128)S(1)} %copy-done.3, f32[8,97]{1,0:T(8,128)S(1)} %copy-done.1, bf16[16,65632]{1,0:T(8,128)(2,1)S(1)} %copy-done), custom_call_target="tpu_custom_call" | custom-call | tf_op jit(solution)/shard_map/column_means/pallas_call | solution.py:266
  18.7 0.3 fusion.5
  19.0 0.3 fusion.7
  19.3 0.0 copy-start.2
  19.3 0.1 copy.8
  19.4 0.4 copy.7
  19.8 50.0 %gather_correlate.1.acc_ref = f32[1024,256]{1,0:T(8,128)S(1)} custom-call(bf16[128,16,128]{2,1,0:T(8,128)(2,1)S(1)} %bitcast.8, bf16[3072,128]{1,0:T(8,128)(2,1)S(1)} %get-tuple-element.8.x_ref), custom_call_target="tpu_custom_call" | custom-call | tf_op jit(solution)/shard_map/gather_correlate/pallas_call | solution.py:441
  69.8 0.0 copy-done.2
  69.8 1.9 %place.1 = f32[256,1024]{1,0:T(8,128)} custom-call(s32[1,256]{1,0:T(1,128)S(1)} %bitcast.11, f32[1024,256]{1,0:T(8,128)S(1)} %gather_correlate.1.acc_ref), custom_call_target="tpu_custom_call" | custom-call | tf_op jit(solution)/shard_map/place/pallas_call | solution.py:468
  (2 shorter events, 0.0 us)
Async XLA Ops:
  0.0 2.0 %copy-start.1 = (f32[8,97]{1,0:T(8,128)S(1)}, f32[8,97]{1,0:T(8,128)}, u32[]{:S(2)}) copy-start(f32[8,97]{1,0:T(8,128)} %table_ref.1) | copy-start | bytes 9316
  0.0 2.0 %copy-start.3 = (s32[16]{0:T(128)S(1)}, s32[16]{0:T(128)}, u32[]{:S(2)}) copy-start(s32[16]{0:T(128)} %index_ref.1) | copy-start | bytes 196
  0.0 2.1 %copy-start = (bf16[16,65632]{1,0:T(8,128)(2,1)S(1)}, bf16[16,65632]{1,0:T(8,128)(2,1)}, u32[]{:S(2)}) copy-start(bf16[16,65632]{1,0:T(8,128)(2,1)} %templates_ref.1) | copy-start | bytes 6300676
  19.3 50.6 %copy-start.2 = (s32[256]{0:T(256)S(1)}, s32[256]{0:T(256)}, u32[]{:S(2)}) copy-start(s32[256]{0:T(256)} %param.11) | copy-start | bytes 3076
where the time goes:
time: 71.8 us; the launch traced here: 71.7 us
  Pallas kernels  68.4 us (95%)
  other arithmetic  2.6 us (4%)
    pallas_call x1, Pallas kernels, gather_correlate(): pl.pallas_call(functools.partial(gather_kernel, chunks), out_shape=jax.Sh...  50 us
    pallas_call x1, Pallas kernels, column_means(): pl.pallas_call(functools.partial(mean_kernel, n), out_shape=(jax.ShapeDty...  16.6 us
    reduce_sum x1, other arithmetic, shards(): sums, counts = (jnp.sum(flux, axis=0), jnp.sum(present, axis=0))  2 us
    pallas_call x1, Pallas kernels, place(): pl.pallas_call(place_kernel, out_shape=jax.ShapeDtypeStruct((total_rows,...  1.86 us

commit v1 on v0

v1 whole, which is shorter than its diff:
```python
import functools
import math

import jax
import jax.numpy as jnp
from jax import lax
from jax.experimental import pallas as pl
from jax.experimental.pallas import tpu as pltpu
from jax.sharding import PartitionSpec as P

PIX = 16384
LAGS = 64
TAPS = 97
KERNELS = 8
Q = 128
R = PIX // Q
BAND = 640
CHUNKS = 8
LEAD = 3
AHEAD = 7
F32 = jnp.float32
BF16 = jnp.bfloat16
MESH = pl.DeviceIdType.MESH
NT_DIMS = (((1,), (1,)), ((), ()))


def template_kernel(index_ref, table_ref, templates_ref, x_ref, bands, chunks, smooth):
    count = templates_ref.shape[0]
    spread_templates(table_ref, templates_ref, bands, chunks)
    smooth_templates(index_ref, bands, chunks, smooth, 0, count, count)
    pack_templates(smooth, x_ref, count)


def spread_templates(table_ref, templates_ref, bands, chunks):
    count = templates_ref.shape[0]
    for k in range(KERNELS):
        row = jnp.concatenate(
            [table_ref[k : k + 1, :], jnp.zeros((1, BAND - TAPS), F32)], axis=1
        )
        row = jnp.broadcast_to(row, (Q, BAND))
        band = pltpu.roll(row, 0, 1, stride=4, stride_axis=0)
        high = band.astype(BF16)
        bands[k, :, :BAND] = high
        bands[k, :, BAND:] = (band - high.astype(F32)).astype(BF16)

    def spread(r, _):
        at = pl.multiple_of(r * (4 * Q), 128)
        piece = templates_ref[:, pl.ds(at, BAND)].astype(F32)
        for i in range(BAND // 128):
            chunks[i, pl.ds(pl.multiple_of(r * count, count), count), :] = piece[
                :, 128 * i : 128 * (i + 1)
            ]
        return 0

    lax.fori_loop(0, R - 1, spread, 0, unroll=8)
    last = (R - 1) * 4 * Q
    left = templates_ref.shape[1] - last
    tail = templates_ref[:, last:].astype(F32)
    tail = jnp.concatenate([tail, jnp.zeros((count, BAND - left), F32)], axis=1)
    for i in range(BAND // 128):
        chunks[i, (R - 1) * count :, :] = tail[:, 128 * i : 128 * (i + 1)]


def smooth_templates(index_ref, bands, chunks, smooth, first, last, count):
    for t in range(first, last):
        rows = [
            chunks[i, pl.ds(t, R, stride=count), :].astype(BF16) for i in range(BAND // 128)
        ]
        rows = jnp.concatenate(rows + rows, axis=1)
        flux = lax.dot_general(
            bands[index_ref[t]], rows, NT_DIMS, preferred_element_type=F32
        )
        total = jnp.sum(flux * flux)
        smooth[pl.ds(t, Q, stride=count), :] = flux * lax.rsqrt(
            jnp.full((1, 1), total) / PIX + 1e-06
        )


def pack_templates(smooth, x_ref, count):
    half = LAGS // 2
    body = smooth[...]
    lane = lax.broadcasted_iota(jnp.int32, (half * count, R), 1)
    x_ref[half * count : (half + Q) * count, :] = body.astype(BF16)
    before = pltpu.roll(body[(Q - half) * count :, :], 1, 1)
    x_ref[: half * count, :] = jnp.where(lane == 0, 0.0, before).astype(BF16)
    after = pltpu.roll(body[: half * count, :], R - 1, 1)
    x_ref[(half + Q) * count :, :] = jnp.where(lane == R - 1, 0.0, after).astype(BF16)


def shape_templates(templates, template_kernel_index, line_spread_table):
    count = templates.shape[0]
    return pl.pallas_call(
        template_kernel,
        out_shape=jax.ShapeDtypeStruct(((Q + LAGS) * count, R), BF16),
        in_specs=[
            pl.BlockSpec(memory_space=pltpu.SMEM),
            pl.BlockSpec(memory_space=pltpu.VMEM),
            pl.BlockSpec(memory_space=pltpu.VMEM),
        ],
        out_specs=pl.BlockSpec(memory_space=pltpu.VMEM),
        scratch_shapes=[
            pltpu.VMEM((KERNELS, Q, 2 * BAND), BF16),
            pltpu.VMEM((BAND // 128, R * count, 128), F32),
            pltpu.VMEM((Q * count, R), F32),
        ],
        compiler_params=pltpu.CompilerParams(vmem_limit_bytes=40 * 2**20),
        cost_estimate=pl.CostEstimate(
            flops=2 * count * Q * R * 2 * BAND, bytes_accessed=6 * 2**20, transcendentals=0
        ),
        name="shape_templates",
    )(template_kernel_index, line_spread_table, templates)


def place_rows(rows_ref, acc, out_ref, count):
    total_rows = rows_ref.shape[1]
    chosen = (
        lax.broadcasted_iota(jnp.int32, (total_rows, total_rows), 0) == rows_ref[...]
    ).astype(BF16)
    both = jnp.concatenate([chosen, chosen], axis=1)
    for t in range(0, count, 2):
        part = jnp.concatenate(
            [
                jnp.concatenate(
                    [
                        acc[h, pl.ds(t + i, LAGS, stride=count), :]
                        for h in range(total_rows // 128)
                    ],
                    axis=1,
                )
                for i in range(2)
            ],
            axis=0,
        ) * F32(1.0 / math.sqrt(PIX))
        high = part.astype(BF16)
        low = (part - high.astype(F32)).astype(BF16)
        out_ref[:, t * LAGS : (t + 2) * LAGS] = lax.dot_general(
            both,
            jnp.concatenate([high, low], axis=1),
            NT_DIMS,
            preferred_element_type=F32,
        )


def correlate_kernel(step_q, rows_ref, x_ref, g_ref, out_ref, acc):
    step = pl.program_id(0)
    total_rows = rows_ref.shape[1]
    count = x_ref.shape[0] // (Q + LAGS)
    tile = 256

    @pl.when(step == 0)
    def _():
        acc[...] = jnp.zeros_like(acc)

    right = jnp.concatenate([g_ref[i] for i in range(step_q)], axis=1)
    for m in range(LAGS * count // tile):
        left = jnp.concatenate(
            [
                x_ref[pl.ds(pl.multiple_of((step * step_q + i) * count + m * tile, 16), tile), :]
                for i in range(step_q)
            ],
            axis=1,
        )
        part = lax.dot_general(left, right, NT_DIMS, preferred_element_type=F32)
        for h in range(total_rows // 128):
            acc[h, m * tile : (m + 1) * tile, :] += part[:, 128 * h : 128 * (h + 1)]

    @pl.when(step == pl.num_programs(0) - 1)
    def _():
        place_rows(rows_ref, acc, out_ref, count)


def correlate(x, gathered, exposure_per_row):
    total_rows = gathered.shape[1]
    count = x.shape[0] // (Q + LAGS)
    step_q = 8
    return pl.pallas_call(
        functools.partial(correlate_kernel, step_q),
        grid=(Q // step_q,),
        out_shape=jax.ShapeDtypeStruct((total_rows, count * LAGS), F32),
        in_specs=[
            pl.BlockSpec((1, total_rows), lambda s: (0, 0)),
            pl.BlockSpec(x.shape, lambda s: (0, 0)),
            pl.BlockSpec((step_q, total_rows, R), lambda s: (s, 0, 0)),
        ],
        out_specs=pl.BlockSpec((total_rows, count * LAGS), lambda s: (0, 0)),
        scratch_shapes=[pltpu.VMEM((total_rows // 128, LAGS * count, 128), F32)],
        compiler_params=pltpu.CompilerParams(vmem_limit_bytes=40 * 2**20),
        name="correlate",
    )(exposure_per_row.reshape(1, total_rows), x, gathered)


def column_sums(mine, psum):
    kind = lax.broadcasted_iota(jnp.int32, (16, 256), 0)
    lane = lax.broadcasted_iota(jnp.int32, (16, 256), 1)
    pick = (lane // 16 == kind).astype(BF16)
    for j in range(Q // 16):
        part = mine[16 * j : 16 * (j + 1)].reshape(256, R)
        good = (part.astype(F32) > 0).astype(BF16)
        for i, what in enumerate((part, good)):
            psum[j // 4, i, 16 * (j % 4) : 16 * (j % 4 + 1), :] = lax.dot_general(
                pick, what, (((1,), (0,)), ((), ())), preferred_element_type=F32
            )


def row_scales(mine, means):
    zero = jnp.zeros((16, R), F32)

    def add(j, total):
        for i in range(16):
            flux = mine[16 * j + i].astype(F32)
            resid = jnp.where(flux > 0, flux - means[j, i : i + 1, :], 0.0)
            total = total + resid * resid
        return total

    total = lax.fori_loop(0, Q // 16, add, zero)
    return lax.rsqrt(jnp.sum(total, axis=1, keepdims=True) / PIX + 1e-06)


def diagonal():
    row = lax.broadcasted_iota(jnp.int32, (16, R), 0)
    lane = lax.broadcasted_iota(jnp.int32, (16, R), 1)
    return row == lane


def store_body(smooth, x, count):
    x[0, LAGS // 2 : LAGS // 2 + Q] = smooth[...].reshape(Q, count, R).astype(BF16)


def store_margins(x, tt):
    half = LAGS // 2
    count = x.shape[2]
    lane = lax.broadcasted_iota(jnp.int32, (half * count, R), 1)

    def rolled(first, shift, edge):
        part = x[tt, first : first + half].reshape(half * count, R).astype(F32)
        part = jnp.where(lane == edge, 0.0, pltpu.roll(part, shift, 1))
        return part.astype(BF16).reshape(half, count, R)

    x[tt, :half] = rolled(Q, 1, 0)
    x[tt, half + Q :] = rolled(half, R - 1, R - 1)


def cross_kernel(
    mine,
    index_ref,
    table_ref,
    templates_ref,
    out_ref,
    raw,
    ready,
    x,
    partner,
    psum,
    tsum,
    csum,
    rsum,
    means,
    row_scale,
    scale,
    bands,
    chunks,
    smooth,
    raw_send,
    raw_recv,
    x_sem,
    r_send,
    r_recv,
    t_sem,
    s_send,
    s_recv,
    m_send,
    m_recv,
    v_send,
    v_recv,
):
    me = lax.axis_index("blk")
    z, y, c = me // 4, (me // 2) % 2, me % 2
    planes = 4
    count = templates_ref.shape[0]
    span = Q // CHUNKS

    def blk(zz, yy, cc):
        return (zz * 2 + yy) * 2 + cc

    up, down = blk(z + 1, y, c), blk(z - 1, y, c)
    beside, twin = blk(z, 1 - y, c), blk(z, y, 1 - c)
    middle = (z == 1) | (z == 2)
    has_up, has_down = z < planes - 1, z > 0

    def remote(src, dst, send, recv, to):
        return pltpu.make_async_remote_copy(
            src_ref=src,
            dst_ref=dst,
            send_sem=send,
            recv_sem=recv,
            device_id={"blk": to},
            device_id_type=MESH,
        )

    barrier = pltpu.get_barrier_semaphore()

    def greet(o, _):
        pl.semaphore_signal(
            barrier, inc=1, device_id={"blk": lax.rem(me + o, 16)}, device_id_type=MESH
        )
        return 0

    lax.fori_loop(1, 16, greet, 0)
    raw[z, c] = mine[...]
    pl.semaphore_wait(barrier, 15)

    def raw_copy(zs, k, kind, to):
        part = raw.at[zs, c, pl.ds(k * span, span)]
        return remote(
            part, part, raw_send.at[kind, zs, k], raw_recv.at[zs * 2 + c, k], to
        )

    def from_twin(zs, k):
        part = raw.at[zs, 1 - c, pl.ds(k * span, span)]
        remote(
            part, part, raw_send.at[2, zs, k], raw_recv.at[zs * 2 + 1 - c, k], twin
        ).wait_recv()

    def on_sides(h, act):
        for sign in (1, -1):
            zs = z + sign * h
            pl.when((zs >= 0) & (zs < planes))(functools.partial(act, zs, sign))

    def send(s):
        h, k = s // CHUNKS, s % CHUNKS
        if h == 0:
            pl.when(has_up)(lambda: raw_copy(z, k, 0, up).start())
            pl.when(has_down)(lambda: raw_copy(z, k, 1, down).start())
            raw_copy(z, k, 2, twin).start()
        elif h < planes - 1:

            def onward(zs, sign):
                if sign > 0:
                    pl.when(has_down)(lambda: raw_copy(zs, k, 1, down).start())
                else:
                    pl.when(has_up)(lambda: raw_copy(zs, k, 0, up).start())

            on_sides(h, onward)

    def arrive(s):
        h, k = s // CHUNKS + 1, s % CHUNKS

        def land(zs, sign):
            raw_copy(zs, k, 2, twin).wait_recv()
            raw_copy(zs, k, 2, twin).start()

        on_sides(h, land)

    def step(s):
        arrive(s)
        send(s + LEAD)

    for s in range(LEAD):
        send(s)

    column_sums(mine, psum)
    to_twin = remote(psum.at[1 - c], tsum, t_sem.at[0], t_sem.at[1], twin)
    to_twin.start()
    spread_templates(table_ref, templates_ref, bands, chunks)

    def owner(w):
        return blk(1 + w // 2, w % 2, c)

    def sum_copy(w):
        return remote(
            csum.at[w], rsum.at[z * 2 + y], s_send.at[w], s_recv.at[z * 2 + y], owner(w)
        )

    def sum_from(i):
        return remote(csum.at[0], rsum.at[i], s_send.at[0], s_recv.at[i], twin)

    def mean_copy(w, o):
        part = means.at[4 * c + w]
        chip = lax.rem(z * 2 + y + o, 8)
        return remote(
            part, part, m_send.at[o], m_recv.at[w], blk(chip // 2, chip % 2, c)
        )

    mine_w = (z - 1) * 2 + y

    def sums_to_owners():
        to_twin.wait_recv()
        for w in range(4):
            rows = slice(16 * w, 16 * (w + 1))
            csum[w] = psum[c, :, rows, :] + tsum[:, rows, :]
            away = jnp.logical_not(middle & (mine_w == w))
            pl.when(away)(lambda: sum_copy(w).start())

            @pl.when(jnp.logical_not(away))
            def _():
                rsum[z * 2 + y] = csum[w]

    def means_from_owner():
        @pl.when(middle)
        def _():
            for i in range(8):
                pl.when(z * 2 + y != i)(lambda: sum_from(i).wait_recv())
            total = rsum[0]
            for i in range(1, 8):
                total = total + rsum[i]
            means[4 * c + mine_w] = total[0] / jnp.maximum(total[1], 1.0)
            for o in range(1, 8):
                mean_copy(mine_w, o).start()

    half_means = remote(
        means.at[pl.ds(4 * c, 4)],
        means.at[pl.ds(4 * c, 4)],
        t_sem.at[2],
        t_sem.at[3],
        twin,
    )

    def means_to_twin():
        for w in range(4):
            away = jnp.logical_not(middle & (mine_w == w))
            pl.when(away)(lambda: mean_copy(w, 1).wait_recv())
        half_means.start()

    def scale_copy(o):
        at = lax.rem(z * 2 + c + o, 8)
        return remote(
            row_scale.at[z * 2 + c],
            row_scale.at[z * 2 + c],
            v_send.at[o],
            v_recv.at[z * 2 + c],
            blk(at // 2, y, at % 2),
        )

    def scales_out():
        half_means.wait_recv()
        own = row_scales(mine, means)
        row_scale[z * 2 + c] = jnp.sum(
            jnp.where(diagonal(), own, 0.0), axis=0, keepdims=True
        )
        for o in range(1, 8):
            scale_copy(o).start()

    def scales_in():
        for i in range(8):
            part = row_scale.at[i]
            pl.when(z * 2 + c != i)(
                lambda: remote(part, part, v_send.at[0], v_recv.at[i], twin).wait_recv()
            )
            column = jnp.sum(
                jnp.where(diagonal(), row_scale[i], 0.0), axis=1, keepdims=True
            )
            scale[i] = jnp.broadcast_to(column, (16, R))

    x_copy = remote(
        x.at[0, pl.ds(LAGS // 2, Q)],
        x.at[1, pl.ds(LAGS // 2, Q)],
        x_sem.at[0],
        x_sem.at[1],
        beside,
    )

    after = {2: sums_to_owners, 8: means_from_owner, 12: means_to_twin}
    for t in range(0, count, 2):
        smooth_templates(index_ref, bands, chunks, smooth, t, t + 2, count)
        step(t // 2)
        after.get(t + 2, lambda: None)()
    store_body(smooth, x, count)
    x_copy.start()
    scales_out()
    for zs in range(planes):
        ready[zs, :AHEAD] = jnp.zeros((AHEAD, 32, R), BF16)
        ready[zs, AHEAD + Q :] = jnp.zeros((ready.shape[1] - AHEAD - Q, 32, R), BF16)
    store_margins(x, 0)
    step(8)

    def normalise(zs, first, last):
        for cc in range(2):
            factor = scale[zs * 2 + cc]

            def tile(j, _):
                for i in range(16):
                    flux = raw[zs, cc, 16 * j + i].astype(F32)
                    resid = jnp.where(flux > 0, flux - means[j, i : i + 1, :], 0.0)
                    ready[zs, AHEAD + 16 * j + i, 16 * cc : 16 * (cc + 1), :] = (
                        resid * factor
                    ).astype(BF16)
                return 0

            lax.fori_loop(first, last, tile, 0)

    def product(zs, quarter):
        first = 32 * quarter
        width = 32 if quarter < 3 else 40
        right = jnp.concatenate(
            [ready[zs, first + i : first + i + 8].reshape(256, R) for i in range(width)],
            axis=1,
        )
        left = jnp.concatenate(
            [
                jnp.concatenate(
                    [x[tt, first + i + 8 * a] for tt in range(2) for a in range(8)], axis=0
                )
                for i in range(width)
            ],
            axis=1,
        )
        part = lax.dot_general(left, right, NT_DIMS, preferred_element_type=F32)
        if quarter == 0:
            out_ref[zs * 2 + y] = part[:128]
            partner[zs] = part[128:]
        else:
            out_ref[zs * 2 + y] += part[:128]
            partner[zs] += part[128:]

    def result_copy(zs):
        return remote(
            partner.at[zs], out_ref.at[zs * 2 + y], r_send.at[zs], r_recv.at[zs], beside
        )

    def slot(i):
        if isinstance(i, int) and i == 3:
            return jnp.where(z < 2, 3, 0)
        near = jnp.where(z < 2, z + 1, z - 1)
        far = jnp.where(z == 0, 2, jnp.where(z == 1, 0, jnp.where(z == 2, 3, 1)))
        return jnp.where(i == 0, z, jnp.where(i == 1, near, far))

    def all_from_twin(zs):
        for k in range(CHUNKS):
            from_twin(zs, k)

    def whole(i, _):
        zs = slot(i)
        for quarter in range(4):
            product(zs, quarter)
        result_copy(zs).start()
        return 0

    def prepare(i):
        all_from_twin(slot(i))
        normalise(slot(i), 0, Q // 16)

    step(9)
    step(10)
    scales_in()
    prepare(0)
    step(11)
    prepare(1)
    for s in range(12, 16):
        step(s)
    x_copy.wait_recv()
    store_margins(x, 1)
    lax.fori_loop(0, 2, whole, 0)
    prepare(2)
    lax.fori_loop(2, 3, whole, 0)
    last = slot(3)
    for quarter in range(4):
        for s in range(16 + 2 * quarter, 18 + 2 * quarter):
            step(s)
        for k in range(2 * quarter, 2 * quarter + 2):
            from_twin(last, k)
        normalise(last, 2 * quarter, 2 * quarter + 2)
        product(last, quarter)
    result_copy(last).start()

    x_copy.wait_send()
    to_twin.wait_send()
    half_means.wait_send()
    for w in range(4):
        away = jnp.logical_not(middle & (mine_w == w))
        pl.when(away)(lambda: sum_copy(w).wait_send())

    @pl.when(middle)
    def _():
        for o in range(1, 8):
            mean_copy(mine_w, o).wait_send()

    for o in range(1, 8):
        scale_copy(o).wait_send()

    def sent(k, _):
        for zs in range(planes):
            raw_copy(zs, k, 2, twin).wait_send()
            pl.when(has_up & (zs <= z))(lambda: raw_copy(zs, k, 0, up).wait_send())
            pl.when(has_down & (zs >= z))(lambda: raw_copy(zs, k, 1, down).wait_send())
        return 0

    lax.fori_loop(0, CHUNKS, sent, 0)
    for zs in range(planes):
        result_copy(zs).wait_send()
    for zs in range(planes):
        result_copy(zs).wait_recv()


def cross(masked, templates, template_kernel_index, line_spread_table):
    count = templates.shape[0]
    rows = masked.shape[1]
    vmem = pl.BlockSpec(memory_space=pltpu.VMEM)
    dma = pltpu.SemaphoreType.DMA
    return pl.pallas_call(
        cross_kernel,
        out_shape=jax.ShapeDtypeStruct((8, 8 * count, 256), F32),
        in_specs=[vmem, pl.BlockSpec(memory_space=pltpu.SMEM), vmem, vmem],
        out_specs=vmem,
        scratch_shapes=[
            pltpu.VMEM((4, 2, Q, rows, R), BF16),
            pltpu.VMEM((4, Q + 16, 2 * rows, R), BF16),
            pltpu.VMEM((2, Q + LAGS, count, R), BF16),
            pltpu.VMEM((4, 8 * count, 256), F32),
            pltpu.VMEM((2, 2, Q // 2, R), F32),
            pltpu.VMEM((2, Q // 2, R), F32),
            pltpu.VMEM((4, 2, 16, R), F32),
            pltpu.VMEM((8, 2, 16, R), F32),
            pltpu.VMEM((8, 16, R), F32),
            pltpu.VMEM((8, 1, R), F32),
            pltpu.VMEM((8, 16, R), F32),
            pltpu.VMEM((KERNELS, Q, 2 * BAND), BF16),
            pltpu.VMEM((BAND // 128, R * count, 128), F32),
            pltpu.VMEM((Q * count, R), F32),
            dma((3, 4, CHUNKS)),
            dma((8, CHUNKS)),
            dma((2,)),
            dma((4,)),
            dma((4,)),
            dma((4,)),
            dma((4,)),
            dma((8,)),
            dma((8,)),
            dma((4,)),
            dma((8,)),
            dma((8,)),
        ],
        compiler_params=pltpu.CompilerParams(
            collective_id=0, has_side_effects=True, vmem_limit_bytes=48 * 2**20
        ),
        name="cross",
    )(masked, template_kernel_index, line_spread_table, templates)


def place_kernel(rows_ref, part_ref, out_ref, split):
    count = part_ref.shape[1] // 8
    lane = lax.broadcasted_iota(jnp.int32, (8 * count, 128), 1) // 32
    for h in range(2):
        for b in range(8):
            at = 7 - b
            piece = None
            for i in range(4):
                one = part_ref[4 * h + i, :, 128 * (at // 4) : 128 * (at // 4 + 1)]
                shift = 32 * (i - at % 4) % 128
                one = pltpu.roll(one, shift, 1) if shift else one
                piece = one if piece is None else jnp.where(lane == i, one, piece)
            for a in range(8):
                split[h, (8 * a + b) * count : (8 * a + b + 1) * count, :] = piece[
                    a * count : (a + 1) * count
                ]
    place_rows(rows_ref, split, out_ref, count)


def place(parts, exposure_per_row):
    total_rows = 32 * parts.shape[0]
    across = parts.shape[1] * 8
    return pl.pallas_call(
        place_kernel,
        out_shape=jax.ShapeDtypeStruct((total_rows, across), F32),
        in_specs=[pl.BlockSpec(memory_space=pltpu.VMEM)] * 2,
        out_specs=pl.BlockSpec(memory_space=pltpu.VMEM),
        scratch_shapes=[pltpu.VMEM((total_rows // 128, across, 128), F32)],
        compiler_params=pltpu.CompilerParams(vmem_limit_bytes=16 * 2**20),
        name="place",
    )(exposure_per_row.reshape(1, total_rows), parts)


def shards(
    devices,
    observed,
    good_pixel_mask,
    templates,
    template_kernel_index,
    line_spread_table,
    exposure_per_row,
):
    rows = observed.shape[0]
    flux = jnp.where(good_pixel_mask > 0, observed, 0)
    if devices == 16 and rows == 16 and templates.shape[0] == 16:
        masked = flux.reshape(rows, R, Q).transpose(2, 0, 1)
        parts = cross(masked, templates, template_kernel_index, line_spread_table)
        return place(parts, exposure_per_row)
    flux = flux.astype(F32)
    present = (flux > 0).astype(F32)
    sums, counts = jnp.sum(flux, axis=0), jnp.sum(present, axis=0)
    x = shape_templates(templates, template_kernel_index, line_spread_table)
    sums = lax.psum(jnp.stack([sums, counts]), "blk")
    mean = sums[0] / jnp.maximum(sums[1], 1.0)
    resid = present * (flux - mean[None, :])
    scale = lax.rsqrt(jnp.sum(resid * resid, axis=1) / PIX + 1e-06)
    ready = (resid * scale[:, None]).astype(BF16)
    ready = ready.reshape(rows, R, Q).transpose(2, 0, 1)
    gathered = lax.all_gather(ready, "blk", axis=1, tiled=True)
    return correlate(x, gathered, exposure_per_row)


def solution(mesh):
    in_specs = (
        P(("grp", "blk"), None),
        P(("grp", "blk"), None),
        P(("grp", "blk"), None),
        P(("grp", "blk")),
        P(),
        P("grp"),
    )
    out_specs = P("grp", "blk")
    return jax.shard_map(
        functools.partial(shards, mesh.shape["blk"]),
        mesh=mesh,
        in_specs=in_specs,
        out_specs=out_specs,
        check_vma=False,
    )
```

time: 71.8 us -> 67.3 us (0.937)
  Pallas kernels: 68.4 us -> 64.8 us
  other arithmetic: 2.6 us -> 1.65 us
    pallas_call x2 -> x1, Pallas kernels: 66.6 us -> 62.4 us  [cross(): pl.pallas_call(cross_kernel, out_shape=jax.ShapeDtypeStruct((8, 8 * count...]
    reduce_sum x2 -> x0, other arithmetic: 2.32 us -> none  [the longest x1 2 us: shards(): sums, counts = (jnp.sum(flux, axis=0), jnp.sum(present, axis=0))]
    unnamed x1, other arithmetic: 0.26 us -> 1.65 us
where the time goes in v1:
time: 67.3 us; the launch traced here: 67.1 us
  Pallas kernels  64.8 us (96%)
  other arithmetic  1.65 us (2%)
    pallas_call x1, Pallas kernels, cross(): pl.pallas_call(cross_kernel, out_shape=jax.ShapeDtypeStruct((8, 8 * count...  62.4 us
    pallas_call x1, Pallas kernels, place(): pl.pallas_call(place_kernel, out_shape=jax.ShapeDtypeStruct((total_rows,...  2.49 us
    unnamed x1, other arithmetic  1.65 us

profile of v1, /device:TPU:0, one launch (start us, length us, event | category | flops | bytes accessed | tf_op | source)
XLA Modules:
  0.0 67.1 jit_solution(3042911816465809691)
XLA Ops:
  0.0 0.0 copy-start.1
  0.0 0.0 copy-start.3
  0.0 0.0 copy-start
  0.0 1.7 %fusion = bf16[2,8,128,128]{3,1,2,0:T(8,128)(2,1)S(1)} fusion(bf16[16,16384]{1,0:T(8,128)(2,1)} %param.6, s32[16,16384]{1,0:T(8,128)} %param.7), kind=kLoop, calls=%fused_computation.1 | loop fusion | flops 524288 | bytes 2097152
  1.7 0.1 copy.8
  1.8 0.4 copy.7
  2.2 0.0 copy-start.2
  2.2 0.0 copy-done.1
  2.2 0.0 copy-done.3
  2.2 0.0 copy-done
  2.2 62.4 %cross.1.part_ref = f32[8,128,256]{2,1,0:T(8,128)S(1)} custom-call(bf16[128,16,128]{2,1,0:T(8,128)(2,1)S(1)} %bitcast.5, s32[16]{0:T(128)S(1)} %copy-done.3, f32[8,97]{1,0:T(8,128)S(1)} %copy-done.1, bf16[16,65632]{1,0:T(8,128)(2,1)S(1)} %copy-done), custom_call_target="tpu_custom_call" | custom-call | tf_op jit(solution)/shard_map/cross/pallas_call | solution.py:599
  64.6 0.0 copy-done.2
  64.6 2.5 %place.1 = f32[256,1024]{1,0:T(8,128)} custom-call(s32[1,256]{1,0:T(1,128)S(1)} %bitcast.6, f32[8,128,256]{2,1,0:T(8,128)S(1)} %cross.1.part_ref), custom_call_target="tpu_custom_call" | custom-call | tf_op jit(solution)/shard_map/place/pallas_call | solution.py:661
Async XLA Ops:
  0.0 2.2 %copy-start.1 = (f32[8,97]{1,0:T(8,128)S(1)}, f32[8,97]{1,0:T(8,128)}, u32[]{:S(2)}) copy-start(f32[8,97]{1,0:T(8,128)} %table_ref.1) | copy-start | bytes 9316
  0.0 2.2 %copy-start.3 = (s32[16]{0:T(128)S(1)}, s32[16]{0:T(128)}, u32[]{:S(2)}) copy-start(s32[16]{0:T(128)} %index_ref.1) | copy-start | bytes 196
  0.0 2.2 %copy-start = (bf16[16,65632]{1,0:T(8,128)(2,1)S(1)}, bf16[16,65632]{1,0:T(8,128)(2,1)}, u32[]{:S(2)}) copy-start(bf16[16,65632]{1,0:T(8,128)(2,1)} %templates_ref.1) | copy-start | bytes 6300676
  2.2 62.4 %copy-start.2 = (s32[256]{0:T(256)S(1)}, s32[256]{0:T(256)}, u32[]{:S(2)}) copy-start(s32[256]{0:T(256)} %param.11) | copy-start | bytes 3076

commit v2 on v1

--- a/solution.py
+++ b/solution.py
@@ -351,12 +351,12 @@
 
         on_sides(h, land)
 
-    def step(s):
+    def step(s, lead):
         arrive(s)
-        send(s + LEAD)
-
-    for s in range(LEAD):
-        send(s)
+        send(s + lead)
+
+    send(0)
+    send(1)
 
     column_sums(mine, psum)
     to_twin = remote(psum.at[1 - c], tsum, t_sem.at[0], t_sem.at[1], twin)
@@ -451,27 +451,30 @@
             )
             scale[i] = jnp.broadcast_to(column, (16, R))
 
-    x_copy = remote(
-        x.at[0, pl.ds(LAGS // 2, Q)],
-        x.at[1, pl.ds(LAGS // 2, Q)],
-        x_sem.at[0],
-        x_sem.at[1],
-        beside,
-    )
-
-    after = {2: sums_to_owners, 8: means_from_owner, 12: means_to_twin}
-    for t in range(0, count, 2):
-        smooth_templates(index_ref, bands, chunks, smooth, t, t + 2, count)
-        step(t // 2)
-        after.get(t + 2, lambda: None)()
+    def x_copy(k):
+        rows = pl.ds(LAGS // 2 + k * span, span)
+        return remote(
+            x.at[0, rows], x.at[1, rows], x_sem.at[0, k], x_sem.at[1, k], beside
+        )
+
+    smooth_templates(index_ref, bands, chunks, smooth, 0, 2, count)
+    sums_to_owners()
+    send(2)
+    smooth_templates(index_ref, bands, chunks, smooth, 2, count, count)
     store_body(smooth, x, count)
-    x_copy.start()
-    scales_out()
+    x_copy(0).start()
     for zs in range(planes):
         ready[zs, :AHEAD] = jnp.zeros((AHEAD, 32, R), BF16)
         ready[zs, AHEAD + Q :] = jnp.zeros((ready.shape[1] - AHEAD - Q, 32, R), BF16)
     store_margins(x, 0)
-    step(8)
+    after = {3: means_from_owner, 6: means_to_twin, 7: scales_out, 11: scales_in}
+    for s in range(12):
+        step(s, LEAD)
+        if 0 < s + 1 < CHUNKS:
+            x_copy(s + 1).start()
+        after.get(s, lambda: None)()
+    for s in range(12 + LEAD, 20):
+        send(s)
 
     def normalise(zs, first, last):
         for cc in range(2):
@@ -518,51 +521,56 @@
         )
 
     def slot(i):
-        if isinstance(i, int) and i == 3:
-            return jnp.where(z < 2, 3, 0)
         near = jnp.where(z < 2, z + 1, z - 1)
         far = jnp.where(z == 0, 2, jnp.where(z == 1, 0, jnp.where(z == 2, 3, 1)))
-        return jnp.where(i == 0, z, jnp.where(i == 1, near, far))
-
-    def all_from_twin(zs):
-        for k in range(CHUNKS):
-            from_twin(zs, k)
-
-    def whole(i, _):
+        end = jnp.where(z < 2, 3, 0)
+        return jnp.where(
+            i == 0, z, jnp.where(i == 1, near, jnp.where(i == 2, far, end))
+        )
+
+    def block(i, _):
         zs = slot(i)
+
+        @pl.when(i == 0)
+        def _():
+            for k in range(CHUNKS):
+                x_copy(k).wait_recv()
+            store_margins(x, 1)
+
+        @pl.when(i == 1)
+        def _():
+            for s in range(12, 14):
+                step(s, 8)
+
+        @pl.when(i == 2)
+        def _():
+            for s in range(14, 16):
+                step(s, 8)
+
+        @pl.when(i < 3)
+        def _():
+            for k in range(CHUNKS):
+                from_twin(zs, k)
+            normalise(zs, 0, Q // 16)
+
         for quarter in range(4):
-            product(zs, quarter)
+
+            @pl.when(i == 3)
+            def _():
+                for s in range(16 + 2 * quarter, 18 + 2 * quarter):
+                    arrive(s)
+                for k in range(2 * quarter, 2 * quarter + 2):
+                    from_twin(zs, k)
+                normalise(zs, 2 * quarter, 2 * quarter + 2)
+
+            pl.when(z < planes)(functools.partial(product, zs, quarter))
         result_copy(zs).start()
         return 0
 
-    def prepare(i):
-        all_from_twin(slot(i))
-        normalise(slot(i), 0, Q // 16)
-
-    step(9)
-    step(10)
-    scales_in()
-    prepare(0)
-    step(11)
-    prepare(1)
-    for s in range(12, 16):
-        step(s)
-    x_copy.wait_recv()
-    store_margins(x, 1)
-    lax.fori_loop(0, 2, whole, 0)
-    prepare(2)
-    lax.fori_loop(2, 3, whole, 0)
-    last = slot(3)
-    for quarter in range(4):
-        for s in range(16 + 2 * quarter, 18 + 2 * quarter):
-            step(s)
-        for k in range(2 * quarter, 2 * quarter + 2):
-            from_twin(last, k)
-        normalise(last, 2 * quarter, 2 * quarter + 2)
-        product(last, quarter)
-    result_copy(last).start()
-
-    x_copy.wait_send()
+    lax.fori_loop(0, planes, block, 0)
+
+    for k in range(CHUNKS):
+        x_copy(k).wait_send()
     to_twin.wait_send()
     half_means.wait_send()
     for w in range(4):
@@ -618,7 +626,7 @@
             pltpu.VMEM((Q * count, R), F32),
             dma((3, 4, CHUNKS)),
             dma((8, CHUNKS)),
-            dma((2,)),
+            dma((2, CHUNKS)),
             dma((4,)),
             dma((4,)),
             dma((4,)),

time: 67.3 us -> 59.1 us (0.88)
  Pallas kernels: 64.8 us -> 56.7 us
    pallas_call x1, Pallas kernels: 62.4 us -> 54.2 us  [cross(): pl.pallas_call(cross_kernel, out_shape=jax.ShapeDtypeStruct((8, 8 * count...]
where the time goes in v2:
time: 59.1 us; the launch traced here: 59 us
  Pallas kernels  56.7 us (96%)
  other arithmetic  1.65 us (3%)
    pallas_call x1, Pallas kernels, cross(): pl.pallas_call(cross_kernel, out_shape=jax.ShapeDtypeStruct((8, 8 * count...  54.2 us
    pallas_call x1, Pallas kernels, place(): pl.pallas_call(place_kernel, out_shape=jax.ShapeDtypeStruct((total_rows,...  2.49 us
    unnamed x1, other arithmetic  1.65 us

profile of v2, /device:TPU:0, one launch (start us, length us, event | category | flops | bytes accessed | tf_op | source)
XLA Modules:
  0.0 59.0 jit_solution(4766224252157187421)
XLA Ops:
  0.0 0.0 copy-start.1
  0.0 0.0 copy-start.3
  0.0 0.0 copy-start
  0.0 1.7 %fusion = bf16[2,8,128,128]{3,1,2,0:T(8,128)(2,1)S(1)} fusion(bf16[16,16384]{1,0:T(8,128)(2,1)} %param.6, s32[16,16384]{1,0:T(8,128)} %param.7), kind=kLoop, calls=%fused_computation.1 | loop fusion | flops 524288 | bytes 2097152
  1.7 0.1 copy.8
  1.8 0.4 copy.7
  2.2 0.0 copy-start.2
  2.2 0.0 copy-done.1
  2.2 0.0 copy-done.3
  2.2 0.0 copy-done
  2.2 54.2 %cross.1.part_ref = f32[8,128,256]{2,1,0:T(8,128)S(1)} custom-call(bf16[128,16,128]{2,1,0:T(8,128)(2,1)S(1)} %bitcast.5, s32[16]{0:T(128)S(1)} %copy-done.3, f32[8,97]{1,0:T(8,128)S(1)} %copy-done.1, bf16[16,65632]{1,0:T(8,128)(2,1)S(1)} %copy-done), custom_call_target="tpu_custom_call" | custom-call | tf_op jit(solution)/shard_map/cross/pallas_call | solution.py:607
  56.5 0.0 copy-done.2
  56.5 2.5 %place.1 = f32[256,1024]{1,0:T(8,128)} custom-call(s32[1,256]{1,0:T(1,128)S(1)} %bitcast.6, f32[8,128,256]{2,1,0:T(8,128)S(1)} %cross.1.part_ref), custom_call_target="tpu_custom_call" | custom-call | tf_op jit(solution)/shard_map/place/pallas_call | solution.py:669
Async XLA Ops:
  0.0 2.2 %copy-start.1 = (f32[8,97]{1,0:T(8,128)S(1)}, f32[8,97]{1,0:T(8,128)}, u32[]{:S(2)}) copy-start(f32[8,97]{1,0:T(8,128)} %table_ref.1) | copy-start | bytes 9316
  0.0 2.2 %copy-start.3 = (s32[16]{0:T(128)S(1)}, s32[16]{0:T(128)}, u32[]{:S(2)}) copy-start(s32[16]{0:T(128)} %index_ref.1) | copy-start | bytes 196
  0.0 2.2 %copy-start = (bf16[16,65632]{1,0:T(8,128)(2,1)S(1)}, bf16[16,65632]{1,0:T(8,128)(2,1)}, u32[]{:S(2)}) copy-start(bf16[16,65632]{1,0:T(8,128)(2,1)} %templates_ref.1) | copy-start | bytes 6300676
  2.2 54.3 %copy-start.2 = (s32[256]{0:T(256)S(1)}, s32[256]{0:T(256)}, u32[]{:S(2)}) copy-start(s32[256]{0:T(256)} %param.11) | copy-start | bytes 3076

commit v3 on v2

--- a/solution.py
+++ b/solution.py
@@ -16,8 +16,9 @@
 R = PIX // Q
 BAND = 640
 CHUNKS = 8
-LEAD = 3
+LEAD = 4
 AHEAD = 7
+PIECES = ((0, 4), (4, 7), (7, 8))
 F32 = jnp.float32
 BF16 = jnp.bfloat16
 MESH = pl.DeviceIdType.MESH
@@ -272,6 +273,8 @@
     m_recv,
     v_send,
     v_recv,
+    tail,
+    tail_sem,
 ):
     me = lax.axis_index("blk")
     z, y, c = me // 4, (me // 2) % 2, me % 2
@@ -460,6 +463,7 @@
     smooth_templates(index_ref, bands, chunks, smooth, 0, 2, count)
     sums_to_owners()
     send(2)
+    send(3)
     smooth_templates(index_ref, bands, chunks, smooth, 2, count, count)
     store_body(smooth, x, count)
     x_copy(0).start()
@@ -467,13 +471,13 @@
         ready[zs, :AHEAD] = jnp.zeros((AHEAD, 32, R), BF16)
         ready[zs, AHEAD + Q :] = jnp.zeros((ready.shape[1] - AHEAD - Q, 32, R), BF16)
     store_margins(x, 0)
-    after = {3: means_from_owner, 6: means_to_twin, 7: scales_out, 11: scales_in}
-    for s in range(12):
+    after = {2: means_from_owner, 5: means_to_twin, 6: scales_out, 9: scales_in}
+    for s in range(10):
         step(s, LEAD)
         if 0 < s + 1 < CHUNKS:
             x_copy(s + 1).start()
         after.get(s, lambda: None)()
-    for s in range(12 + LEAD, 20):
+    for s in range(10 + LEAD, 18):
         send(s)
 
     def normalise(zs, first, last):
@@ -491,24 +495,24 @@
 
             lax.fori_loop(first, last, tile, 0)
 
-    def product(zs, quarter):
-        first = 32 * quarter
-        width = 32 if quarter < 3 else 40
+    def product(zs, first, last, ends=False):
         right = jnp.concatenate(
-            [ready[zs, first + i : first + i + 8].reshape(256, R) for i in range(width)],
-            axis=1,
+            [ready[zs, i : i + 8].reshape(256, R) for i in range(first, last)], axis=1
         )
         left = jnp.concatenate(
             [
                 jnp.concatenate(
-                    [x[tt, first + i + 8 * a] for tt in range(2) for a in range(8)], axis=0
+                    [x[tt, i + 8 * a] for tt in range(2) for a in range(8)], axis=0
                 )
-                for i in range(width)
+                for i in range(first, last)
             ],
             axis=1,
         )
         part = lax.dot_general(left, right, NT_DIMS, preferred_element_type=F32)
-        if quarter == 0:
+        if ends:
+            out_ref[zs * 2 + y] += part[:128]
+            tail[0] = part[128:].astype(BF16)
+        elif first == 0:
             out_ref[zs * 2 + y] = part[:128]
             partner[zs] = part[128:]
         else:
@@ -539,7 +543,7 @@
 
         @pl.when(i == 1)
         def _():
-            for s in range(12, 14):
+            for s in range(10, 14):
                 step(s, 8)
 
         @pl.when(i == 2)
@@ -547,27 +551,33 @@
             for s in range(14, 16):
                 step(s, 8)
 
-        @pl.when(i < 3)
+        for k in range(CHUNKS):
+            from_twin(zs, k)
+        normalise(zs, 0, Q // 16)
+
+        @pl.when(z < planes)
         def _():
-            for k in range(CHUNKS):
-                from_twin(zs, k)
-            normalise(zs, 0, Q // 16)
-
-        for quarter in range(4):
-
-            @pl.when(i == 3)
-            def _():
-                for s in range(16 + 2 * quarter, 18 + 2 * quarter):
-                    arrive(s)
-                for k in range(2 * quarter, 2 * quarter + 2):
-                    from_twin(zs, k)
-                normalise(zs, 2 * quarter, 2 * quarter + 2)
-
-            pl.when(z < planes)(functools.partial(product, zs, quarter))
+            for quarter in range(4):
+                product(zs, 32 * quarter, 32 * quarter + (32 if quarter < 3 else 40))
+
         result_copy(zs).start()
         return 0
 
-    lax.fori_loop(0, planes, block, 0)
+    lax.fori_loop(0, 3, block, 0)
+    last = slot(3)
+    for first, end in PIECES:
+        for k in range(first, end):
+            arrive(16 + k)
+        for k in range(first, end):
+            from_twin(last, k)
+        normalise(last, first, end)
+        ends = end == CHUNKS
+        low, high = span * first, span * end + (8 if ends else 0)
+        pl.when(z < planes)(functools.partial(product, last, low, high, ends))
+        if first == PIECES[-2][0]:
+            result_copy(last).start()
+    tail_copy = remote(tail.at[0], tail.at[1], tail_sem.at[0], tail_sem.at[1], beside)
+    tail_copy.start()
 
     for k in range(CHUNKS):
         x_copy(k).wait_send()
@@ -595,8 +605,11 @@
     lax.fori_loop(0, CHUNKS, sent, 0)
     for zs in range(planes):
         result_copy(zs).wait_send()
+    tail_copy.wait_send()
     for zs in range(planes):
         result_copy(zs).wait_recv()
+    tail_copy.wait_recv()
+    out_ref[last * 2 + 1 - y] += tail[1].astype(F32)
 
 
 def cross(masked, templates, template_kernel_index, line_spread_table):
@@ -636,6 +649,8 @@
             dma((4,)),
             dma((8,)),
             dma((8,)),
+            pltpu.VMEM((2, 8 * count, 256), BF16),
+            dma((2,)),
         ],
         compiler_params=pltpu.CompilerParams(
             collective_id=0, has_side_effects=True, vmem_limit_bytes=48 * 2**20

time: 59.1 us -> 56.2 us (0.951)
  Pallas kernels: 56.7 us -> 53.8 us
    pallas_call x1, Pallas kernels: 54.2 us -> 51.3 us  [cross(): pl.pallas_call(cross_kernel, out_shape=jax.ShapeDtypeStruct((8, 8 * count...]
where the time goes in v3:
time: 56.2 us; the launch traced here: 56 us
  Pallas kernels  53.8 us (96%)
  other arithmetic  1.65 us (3%)
    pallas_call x1, Pallas kernels, cross(): pl.pallas_call(cross_kernel, out_shape=jax.ShapeDtypeStruct((8, 8 * count...  51.3 us
    pallas_call x1, Pallas kernels, place(): pl.pallas_call(place_kernel, out_shape=jax.ShapeDtypeStruct((total_rows,...  2.51 us
    unnamed x1, other arithmetic  1.65 us

profile of v3, /device:TPU:0, one launch (start us, length us, event | category | flops | bytes accessed | tf_op | source)
XLA Modules:
  0.0 56.0 jit_solution(15207751891605022231)
XLA Ops:
  0.0 0.0 copy-start.1
  0.0 0.0 copy-start.3
  0.0 0.0 copy-start
  0.0 1.7 %fusion = bf16[2,8,128,128]{3,1,2,0:T(8,128)(2,1)S(1)} fusion(bf16[16,16384]{1,0:T(8,128)(2,1)} %param.6, s32[16,16384]{1,0:T(8,128)} %param.7), kind=kLoop, calls=%fused_computation.1 | loop fusion | flops 524288 | bytes 2097152
  1.7 0.1 copy.8
  1.8 0.4 copy.7
  2.2 0.0 copy-start.2
  2.2 0.0 copy-done.1
  2.2 0.0 copy-done.3
  2.2 0.0 copy-done
  2.2 51.3 %cross.1.part_ref = f32[8,128,256]{2,1,0:T(8,128)S(1)} custom-call(bf16[128,16,128]{2,1,0:T(8,128)(2,1)S(1)} %bitcast.5, s32[16]{0:T(128)S(1)} %copy-done.3, f32[8,97]{1,0:T(8,128)S(1)} %copy-done.1, bf16[16,65632]{1,0:T(8,128)(2,1)S(1)} %copy-done), custom_call_target="tpu_custom_call" | custom-call | tf_op jit(solution)/shard_map/cross/pallas_call | solution.py:620
  53.5 0.0 copy-done.2
  53.5 2.5 %place.1 = f32[256,1024]{1,0:T(8,128)} custom-call(s32[1,256]{1,0:T(1,128)S(1)} %bitcast.6, f32[8,128,256]{2,1,0:T(8,128)S(1)} %cross.1.part_ref), custom_call_target="tpu_custom_call" | custom-call | tf_op jit(solution)/shard_map/place/pallas_call | solution.py:684
Async XLA Ops:
  0.0 2.2 %copy-start.1 = (f32[8,97]{1,0:T(8,128)S(1)}, f32[8,97]{1,0:T(8,128)}, u32[]{:S(2)}) copy-start(f32[8,97]{1,0:T(8,128)} %table_ref.1) | copy-start | bytes 9316
  0.0 2.2 %copy-start.3 = (s32[16]{0:T(128)S(1)}, s32[16]{0:T(128)}, u32[]{:S(2)}) copy-start(s32[16]{0:T(128)} %index_ref.1) | copy-start | bytes 196
  0.0 2.2 %copy-start = (bf16[16,65632]{1,0:T(8,128)(2,1)S(1)}, bf16[16,65632]{1,0:T(8,128)(2,1)}, u32[]{:S(2)}) copy-start(bf16[16,65632]{1,0:T(8,128)(2,1)} %templates_ref.1) | copy-start | bytes 6300676
  2.2 51.3 %copy-start.2 = (s32[256]{0:T(256)S(1)}, s32[256]{0:T(256)}, u32[]{:S(2)}) copy-start(s32[256]{0:T(256)} %param.11) | copy-start | bytes 3076

commit v4 on v3

--- a/solution.py
+++ b/solution.py
@@ -18,7 +18,7 @@
 CHUNKS = 8
 LEAD = 4
 AHEAD = 7
-PIECES = ((0, 4), (4, 7), (7, 8))
+PIECES = ((0, 4), (4, 6), (6, 8))
 F32 = jnp.float32
 BF16 = jnp.bfloat16
 MESH = pl.DeviceIdType.MESH

time: 56.2 us -> 55 us (0.979)
  Pallas kernels: 53.8 us -> 52.6 us
    pallas_call x1, Pallas kernels: 51.3 us -> 50.1 us  [cross(): pl.pallas_call(cross_kernel, out_shape=jax.ShapeDtypeStruct((8, 8 * count...]
where the time goes in v4:
time: 55 us; the launch traced here: 54.9 us
  Pallas kernels  52.6 us (96%)
  other arithmetic  1.65 us (3%)
  local copies, waits for them, and re-layouts  0.55 us (1%)
    pallas_call x1, Pallas kernels, cross(): pl.pallas_call(cross_kernel, out_shape=jax.ShapeDtypeStruct((8, 8 * count...  50.1 us
    pallas_call x1, Pallas kernels, place(): pl.pallas_call(place_kernel, out_shape=jax.ShapeDtypeStruct((total_rows,...  2.52 us
    unnamed x1, other arithmetic  1.65 us

profile of v4, /device:TPU:0, one launch (start us, length us, event | category | flops | bytes accessed | tf_op | source)
XLA Modules:
  0.0 54.9 jit_solution(7320516421581677035)
XLA Ops:
  0.0 0.0 copy-start.1
  0.0 0.0 copy-start.3
  0.0 0.0 copy-start
  0.0 1.7 %fusion = bf16[2,8,128,128]{3,1,2,0:T(8,128)(2,1)S(1)} fusion(bf16[16,16384]{1,0:T(8,128)(2,1)} %param.6, s32[16,16384]{1,0:T(8,128)} %param.7), kind=kLoop, calls=%fused_computation.1 | loop fusion | flops 524288 | bytes 2097152
  1.7 0.1 copy.8
  1.8 0.4 copy.7
  2.2 0.0 copy-start.2
  2.2 0.0 copy-done.1
  2.2 0.0 copy-done.3
  2.2 0.0 copy-done
  2.2 50.1 %cross.1.part_ref = f32[8,128,256]{2,1,0:T(8,128)S(1)} custom-call(bf16[128,16,128]{2,1,0:T(8,128)(2,1)S(1)} %bitcast.5, s32[16]{0:T(128)S(1)} %copy-done.3, f32[8,97]{1,0:T(8,128)S(1)} %copy-done.1, bf16[16,65632]{1,0:T(8,128)(2,1)S(1)} %copy-done), custom_call_target="tpu_custom_call" | custom-call | tf_op jit(solution)/shard_map/cross/pallas_call | solution.py:620
  52.4 0.0 copy-done.2
  52.4 2.5 %place.1 = f32[256,1024]{1,0:T(8,128)} custom-call(s32[1,256]{1,0:T(1,128)S(1)} %bitcast.6, f32[8,128,256]{2,1,0:T(8,128)S(1)} %cross.1.part_ref), custom_call_target="tpu_custom_call" | custom-call | tf_op jit(solution)/shard_map/place/pallas_call | solution.py:684
Async XLA Ops:
  0.0 2.2 %copy-start.1 = (f32[8,97]{1,0:T(8,128)S(1)}, f32[8,97]{1,0:T(8,128)}, u32[]{:S(2)}) copy-start(f32[8,97]{1,0:T(8,128)} %table_ref.1) | copy-start | bytes 9316
  0.0 2.2 %copy-start.3 = (s32[16]{0:T(128)S(1)}, s32[16]{0:T(128)}, u32[]{:S(2)}) copy-start(s32[16]{0:T(128)} %index_ref.1) | copy-start | bytes 196
  0.0 2.2 %copy-start = (bf16[16,65632]{1,0:T(8,128)(2,1)S(1)}, bf16[16,65632]{1,0:T(8,128)(2,1)}, u32[]{:S(2)}) copy-start(bf16[16,65632]{1,0:T(8,128)(2,1)} %templates_ref.1) | copy-start | bytes 6300676
  2.2 50.2 %copy-start.2 = (s32[256]{0:T(256)S(1)}, s32[256]{0:T(256)}, u32[]{:S(2)}) copy-start(s32[256]{0:T(256)} %param.11) | copy-start | bytes 3076

commit v5 on v4

--- a/solution.py
+++ b/solution.py
@@ -112,13 +112,13 @@
     )(template_kernel_index, line_spread_table, templates)
 
 
-def place_rows(rows_ref, acc, out_ref, count):
+def place_rows(rows_ref, acc, out_ref, count, group=0, groups=1):
     total_rows = rows_ref.shape[1]
     chosen = (
         lax.broadcasted_iota(jnp.int32, (total_rows, total_rows), 0) == rows_ref[...]
     ).astype(BF16)
     both = jnp.concatenate([chosen, chosen], axis=1)
-    for t in range(0, count, 2):
+    for t in range(group * count // groups, (group + 1) * count // groups, 2):
         part = jnp.concatenate(
             [
                 jnp.concatenate(
@@ -473,12 +473,13 @@
     store_margins(x, 0)
     after = {2: means_from_owner, 5: means_to_twin, 6: scales_out, 9: scales_in}
     for s in range(10):
-        step(s, LEAD)
+        step(s, LEAD if s < 8 else 8)
         if 0 < s + 1 < CHUNKS:
             x_copy(s + 1).start()
         after.get(s, lambda: None)()
-    for s in range(10 + LEAD, 18):
-        send(s)
+        if s == 7:
+            for e in range(8 + LEAD, 8 + 8):
+                send(e)
 
     def normalise(zs, first, last):
         for cc in range(2):
@@ -535,25 +536,25 @@
     def block(i, _):
         zs = slot(i)
 
+        @pl.when(i == 1)
+        def _():
+            for s in range(10, 14):
+                step(s, 8)
+
+        @pl.when(i == 2)
+        def _():
+            for s in range(14, 16):
+                step(s, 8)
+
+        for k in range(CHUNKS):
+            from_twin(zs, k)
+        normalise(zs, 0, Q // 16)
+
         @pl.when(i == 0)
         def _():
             for k in range(CHUNKS):
                 x_copy(k).wait_recv()
             store_margins(x, 1)
-
-        @pl.when(i == 1)
-        def _():
-            for s in range(10, 14):
-                step(s, 8)
-
-        @pl.when(i == 2)
-        def _():
-            for s in range(14, 16):
-                step(s, 8)
-
-        for k in range(CHUNKS):
-            from_twin(zs, k)
-        normalise(zs, 0, Q // 16)
 
         @pl.when(z < planes)
         def _():
@@ -659,7 +660,7 @@
     )(masked, template_kernel_index, line_spread_table, templates)
 
 
-def place_kernel(rows_ref, part_ref, out_ref, split):
+def place_kernel(rows_ref, part_ref, out_hbm, split, out_ref, sem):
     count = part_ref.shape[1] // 8
     lane = lax.broadcasted_iota(jnp.int32, (8 * count, 128), 1) // 32
     for h in range(2):
@@ -675,7 +676,18 @@
                 split[h, (8 * a + b) * count : (8 * a + b + 1) * count, :] = piece[
                     a * count : (a + 1) * count
                 ]
-    place_rows(rows_ref, split, out_ref, count)
+    groups = sem.shape[0]
+    wide = out_ref.shape[1] // groups
+    copies = []
+    for g in range(groups):
+        place_rows(rows_ref, split, out_ref, count, g, groups)
+        at = pl.ds(g * wide, wide)
+        copies.append(
+            pltpu.make_async_copy(out_ref.at[:, at], out_hbm.at[:, at], sem.at[g])
+        )
+        copies[-1].start()
+    for copy in copies:
+        copy.wait()
 
 
 def place(parts, exposure_per_row):
@@ -685,8 +697,12 @@
         place_kernel,
         out_shape=jax.ShapeDtypeStruct((total_rows, across), F32),
         in_specs=[pl.BlockSpec(memory_space=pltpu.VMEM)] * 2,
-        out_specs=pl.BlockSpec(memory_space=pltpu.VMEM),
-        scratch_shapes=[pltpu.VMEM((total_rows // 128, across, 128), F32)],
+        out_specs=pl.BlockSpec(memory_space=pl.ANY),
+        scratch_shapes=[
+            pltpu.VMEM((total_rows // 128, across, 128), F32),
+            pltpu.VMEM((total_rows, across), F32),
+            pltpu.SemaphoreType.DMA((4,)),
+        ],
         compiler_params=pltpu.CompilerParams(vmem_limit_bytes=16 * 2**20),
         name="place",
     )(exposure_per_row.reshape(1, total_rows), parts)

time: 55 us -> 54.7 us (level)
  no operation moved by 1% of the time
where the time goes in v5:
time: 54.7 us; the launch traced here: 54.5 us
  Pallas kernels  52.3 us (96%)
  other arithmetic  1.65 us (3%)
  local copies, waits for them, and re-layouts  0.55 us (1%)
    pallas_call x1, Pallas kernels, cross(): pl.pallas_call(cross_kernel, out_shape=jax.ShapeDtypeStruct((8, 8 * count...  50 us
    pallas_call x1, Pallas kernels, place(): pl.pallas_call(place_kernel, out_shape=jax.ShapeDtypeStruct((total_rows,...  2.28 us
    unnamed x1, other arithmetic  1.65 us

profile of v5, /device:TPU:0, one launch (start us, length us, event | category | flops | bytes accessed | tf_op | source)
XLA Modules:
  0.0 54.5 jit_solution(7754598287423437618)
XLA Ops:
  0.0 0.0 copy-start.1
  0.0 0.0 copy-start.3
  0.0 0.0 copy-start
  0.0 1.7 %fusion = bf16[2,8,128,128]{3,1,2,0:T(8,128)(2,1)S(1)} fusion(bf16[16,16384]{1,0:T(8,128)(2,1)} %param.6, s32[16,16384]{1,0:T(8,128)} %param.7), kind=kLoop, calls=%fused_computation.1 | loop fusion | flops 524288 | bytes 2097152
  1.7 0.1 copy.8
  1.8 0.4 copy.7
  2.2 0.0 copy-start.2
  2.2 0.0 copy-done.1
  2.2 0.0 copy-done.3
  2.2 0.0 copy-done
  2.2 50.0 %cross.1.part_ref = f32[8,128,256]{2,1,0:T(8,128)S(1)} custom-call(bf16[128,16,128]{2,1,0:T(8,128)(2,1)S(1)} %bitcast.5, s32[16]{0:T(128)S(1)} %copy-done.3, f32[8,97]{1,0:T(8,128)S(1)} %copy-done.1, bf16[16,65632]{1,0:T(8,128)(2,1)S(1)} %copy-done), custom_call_target="tpu_custom_call" | custom-call | tf_op jit(solution)/shard_map/cross/pallas_call | solution.py:621
  52.2 0.0 copy-done.2
  52.3 2.3 %place.1 = f32[256,1024]{1,0:T(8,128)} custom-call(s32[1,256]{1,0:T(1,128)S(1)} %bitcast.6, f32[8,128,256]{2,1,0:T(8,128)S(1)} %cross.1.part_ref), custom_call_target="tpu_custom_call" | custom-call | tf_op jit(solution)/shard_map/place/pallas_call | solution.py:696
Async XLA Ops:
  0.0 2.2 %copy-start.1 = (f32[8,97]{1,0:T(8,128)S(1)}, f32[8,97]{1,0:T(8,128)}, u32[]{:S(2)}) copy-start(f32[8,97]{1,0:T(8,128)} %table_ref.1) | copy-start | bytes 9316
  0.0 2.2 %copy-start.3 = (s32[16]{0:T(128)S(1)}, s32[16]{0:T(128)}, u32[]{:S(2)}) copy-start(s32[16]{0:T(128)} %index_ref.1) | copy-start | bytes 196
  0.0 2.2 %copy-start = (bf16[16,65632]{1,0:T(8,128)(2,1)S(1)}, bf16[16,65632]{1,0:T(8,128)(2,1)}, u32[]{:S(2)}) copy-start(bf16[16,65632]{1,0:T(8,128)(2,1)} %templates_ref.1) | copy-start | bytes 6300676
  2.2 50.0 %copy-start.2 = (s32[256]{0:T(256)S(1)}, s32[256]{0:T(256)}, u32[]{:S(2)}) copy-start(s32[256]{0:T(256)} %param.11) | copy-start | bytes 3076

commit v6 on v5

--- a/solution.py
+++ b/solution.py
@@ -569,9 +569,11 @@
     for first, end in PIECES:
         for k in range(first, end):
             arrive(16 + k)
-        for k in range(first, end):
-            from_twin(last, k)
-        normalise(last, first, end)
+            if k > first:
+                from_twin(last, k - 1)
+                normalise(last, k - 1, k)
+        from_twin(last, end - 1)
+        normalise(last, end - 1, end)
         ends = end == CHUNKS
         low, high = span * first, span * end + (8 if ends else 0)
         pl.when(z < planes)(functools.partial(product, last, low, high, ends))

time: 54.7 us -> 54.8 us (level)
  no operation moved by 1% of the time
where the time goes in v6:
time: 54.8 us; the launch traced here: 54.7 us
  Pallas kernels  52.4 us (96%)
  other arithmetic  1.65 us (3%)
  local copies, waits for them, and re-layouts  0.55 us (1%)
    pallas_call x1, Pallas kernels, cross(): pl.pallas_call(cross_kernel, out_shape=jax.ShapeDtypeStruct((8, 8 * count...  50.2 us
    pallas_call x1, Pallas kernels, place(): pl.pallas_call(place_kernel, out_shape=jax.ShapeDtypeStruct((total_rows,...  2.27 us
    unnamed x1, other arithmetic  1.65 us

profile of v6, /device:TPU:0, one launch (start us, length us, event | category | flops | bytes accessed | tf_op | source)
XLA Modules:
  0.0 54.7 jit_solution(2259488869722686671)
XLA Ops:
  0.0 0.0 copy-start.1
  0.0 0.0 copy-start.3
  0.0 0.0 copy-start
  0.0 1.7 %fusion = bf16[2,8,128,128]{3,1,2,0:T(8,128)(2,1)S(1)} fusion(bf16[16,16384]{1,0:T(8,128)(2,1)} %param.6, s32[16,16384]{1,0:T(8,128)} %param.7), kind=kLoop, calls=%fused_computation.1 | loop fusion | flops 524288 | bytes 2097152
  1.7 0.1 copy.8
  1.8 0.4 copy.7
  2.2 0.0 copy-start.2
  2.2 0.0 copy-done.1
  2.2 0.0 copy-done.3
  2.2 0.0 copy-done
  2.2 50.2 %cross.1.part_ref = f32[8,128,256]{2,1,0:T(8,128)S(1)} custom-call(bf16[128,16,128]{2,1,0:T(8,128)(2,1)S(1)} %bitcast.5, s32[16]{0:T(128)S(1)} %copy-done.3, f32[8,97]{1,0:T(8,128)S(1)} %copy-done.1, bf16[16,65632]{1,0:T(8,128)(2,1)S(1)} %copy-done), custom_call_target="tpu_custom_call" | custom-call | tf_op jit(solution)/shard_map/cross/pallas_call | solution.py:623
  52.4 0.0 copy-done.2
  52.4 2.3 %place.1 = f32[256,1024]{1,0:T(8,128)} custom-call(s32[1,256]{1,0:T(1,128)S(1)} %bitcast.6, f32[8,128,256]{2,1,0:T(8,128)S(1)} %cross.1.part_ref), custom_call_target="tpu_custom_call" | custom-call | tf_op jit(solution)/shard_map/place/pallas_call | solution.py:698
Async XLA Ops:
  0.0 2.2 %copy-start.1 = (f32[8,97]{1,0:T(8,128)S(1)}, f32[8,97]{1,0:T(8,128)}, u32[]{:S(2)}) copy-start(f32[8,97]{1,0:T(8,128)} %table_ref.1) | copy-start | bytes 9316
  0.0 2.2 %copy-start.3 = (s32[16]{0:T(128)S(1)}, s32[16]{0:T(128)}, u32[]{:S(2)}) copy-start(s32[16]{0:T(128)} %index_ref.1) | copy-start | bytes 196
  0.0 2.2 %copy-start = (bf16[16,65632]{1,0:T(8,128)(2,1)S(1)}, bf16[16,65632]{1,0:T(8,128)(2,1)}, u32[]{:S(2)}) copy-start(bf16[16,65632]{1,0:T(8,128)(2,1)} %templates_ref.1) | copy-start | bytes 6300676
  2.2 50.2 %copy-start.2 = (s32[256]{0:T(256)S(1)}, s32[256]{0:T(256)}, u32[]{:S(2)}) copy-start(s32[256]{0:T(256)} %param.11) | copy-start | bytes 3076
